TPU v7x, 32 devices: a whole 2x2x4 slice. The times are simulated.
32 devices in a mesh: dp: 4 (over y, x), expert: 8 (over z, core).
Axes of the slice: x: 2, y: 2, z: 4, core: 2. Of those that a mesh axis runs over, the one named last changes fastest.
Arguments:
- tokens: bfloat16 [4096, 2880], P(('dp', 'expert')), may hold values from -6 to 6
- expert_ids: int32 [4096, 4], P(('dp', 'expert')), may hold values from 0 to 7, all different within a row; in each aligned block of 128 rows (0 to 127, 128 to 255, ...) at most 128 rows name the same one
- gates: bfloat16 [4096, 4], P(('dp', 'expert')), may hold values from 0.099609375 to 1
- w_gate: bfloat16 [8, 2880, 1440], P('expert'), may hold values from -0.109375 to 0.109375
- w_up: bfloat16 [8, 2880, 1440], P('expert'), may hold values from -0.109375 to 0.109375
- w_down: bfloat16 [8, 1440, 2880], P('expert'), may hold values from -0.15625 to 0.15625
Outputs:
- mixed: bfloat16 [4096, 2880], P(('dp', 'expert'))
- expert_load: int32 [8], replicated
Inputs may be any that keep to these rules, and one draw needn't show every extreme that they name: `expert_ids`: each token names 4 different experts. Among the rows of one device (aligned blocks of 128 rows) every expert is named by at most 128 rows, a bound that some block reaches.
All inputs are finite; a program needn't handle non-finite values.
Results may differ from a plain program's by a relative error of at most 0.004.
The roundings to bfloat16 on the way count: a program that leaves them out, or rounds other values in their place, can miss the bound.
Values may be sent and summed in bfloat16 or wider, within the bound.
A program may use at most 192 MiB of HBM per device.

v0:
```python
import jax
import jax.numpy as jnp
from jax import lax
from jax.sharding import PartitionSpec as P

BLOCK = 128


def expert_ffn(rows, gate_mat, up_mat, down_mat):
    gate_val = jnp.dot(rows, gate_mat, preferred_element_type=jnp.float32)
    up_val = jnp.dot(rows, up_mat, preferred_element_type=jnp.float32)
    hidden = (jax.nn.silu(gate_val) * up_val).astype(jnp.bfloat16)
    return jnp.dot(hidden, down_mat, preferred_element_type=jnp.float32)


def shards(tokens, expert_ids, gates, w_gate, w_up, w_down):
    tok_rows = tokens.shape[0]
    width = tokens.shape[1]
    n_experts = lax.axis_size("expert")
    onehot = expert_ids[:, :, None] == jnp.arange(n_experts, dtype=jnp.int32)[None, None, :]
    table = jnp.sum(gates.astype(jnp.float32)[:, :, None] * onehot.astype(jnp.float32), axis=1)
    gate_mat = w_gate[0]
    up_mat = w_up[0]
    down_mat = w_down[0]
    gathered, table_all = (
        lax.all_gather(tokens, "expert", axis=0, tiled=True),
        lax.all_gather(table.astype(jnp.bfloat16), "expert", axis=0, tiled=True),
    )
    group_rows = gathered.shape[0]
    capacity = 8 * tok_rows
    expert = lax.axis_index("expert")
    column = lax.dynamic_index_in_dim(table_all, expert, 1, keepdims=False).astype(jnp.float32)
    routed = column > 0
    position = jnp.cumsum(routed.astype(jnp.int32)) - 1
    count = jnp.sum(routed.astype(jnp.int32))
    target = jnp.where(routed, position, capacity)
    slot_tok = (
        jnp.zeros((capacity,), jnp.int32)
        .at[target]
        .set(jnp.arange(group_rows, dtype=jnp.int32), mode="drop")
    )
    slot_weight = jnp.where(jnp.arange(capacity, dtype=jnp.int32) < count, column[slot_tok], 0.0)
    blocks = (count + BLOCK - 1) // BLOCK

    def per_block(index, partial_value):
        rows_idx = lax.dynamic_slice_in_dim(slot_tok, index * BLOCK, BLOCK)
        weight = lax.dynamic_slice_in_dim(slot_weight, index * BLOCK, BLOCK)
        result = expert_ffn(gathered[rows_idx], gate_mat, up_mat, down_mat)
        return partial_value.at[rows_idx].add(result * weight[:, None])

    partial_value = lax.fori_loop(0, blocks, per_block, jnp.zeros((group_rows, width), jnp.float32))
    mixed = lax.psum_scatter(partial_value, "expert", scatter_dimension=0, tiled=True).astype(
        jnp.bfloat16
    )
    local_load = jnp.sum(onehot.astype(jnp.float32), axis=(0, 1))
    expert_load = lax.psum(local_load, ("dp", "expert")).astype(jnp.int32)
    return (mixed, expert_load)


def solution(mesh):
    placed = (
        P(("dp", "expert"), None),
        P(("dp", "expert"), None),
        P(("dp", "expert"), None),
        P("expert", None, None),
        P("expert", None, None),
        P("expert", None, None),
    )
    return jax.shard_map(
        shards,
        mesh=mesh,
        in_specs=placed,
        out_specs=(P(("dp", "expert"), None), P()),
        check_vma=False,
    )
```

profile of v0, /device:TPU:0, one launch (start us, length us, event | category | flops | bytes accessed | tf_op | source)
XLA Modules:
  0.0 532.6 jit_solution(3584806823972242418)
XLA Ops:
  7.2 0.0 all-gather.2.cloned.1.call-start
  7.2 2.3 copy.22
  9.5 0.0 all-gather.2.cloned.1.call-update
  9.5 0.0 reduce-scatter.2.cloned.1.call-start
  9.5 0.7 convert_element_type.40
  10.2 0.8 convert_reduce_fusion
  11.0 14.5 %all_gather.6 = bf16[1024,8]{0,1:T(8,128)(2,1)S(1)} all-gather(bf16[128,8]{0,1:T(8,128)(2,1)S(1)} %get-tuple-element.52), channel_id=1, replica_groups=mesh['dp'=4,'expert'=8] {'expert'}, dimensions={0}, use_global_device_ids=true | all-gather | bytes 18432 | tf_op jit(solution)/shard_map/all_gather | solution.py:27
  25.5 0.6 convert_reduce_fusion.1
  26.8 0.3 reduce-window.9
  27.1 0.1 slice.7
  27.2 0.1 slice_reduce_fusion
  27.3 0.1 add_add_fusion
  27.4 4.3 scatter_custom_fusion.1
  31.8 4.5 gather_fusion.1
  36.3 11.8 %copy.23 = bf16[1,2880,1440]{2,1,0:T(8,128)(2,1)} copy(bf16[1,2880,1440]{1,2,0:T(8,128)(2,1)} %param.11) | data formatting | bytes 16588800 | tf_op args[3]
  48.1 11.8 %copy.24 = bf16[1,2880,1440]{2,1,0:T(8,128)(2,1)} copy(bf16[1,2880,1440]{1,2,0:T(8,128)(2,1)} %param.12) | data formatting | bytes 16588800 | tf_op args[4]
  59.9 0.6 fusion.4
  60.6 14.5 %all-gather.2.cloned.1.call-done = bf16[1024,2880]{1,0:T(8,128)(2,1)} async-done(((bf16[128,2880]{1,0:T(8,128)(2,1)}), bf16[1024,2880]{1,0:T(8,128)(2,1)}) %all-gather.2.cloned.1.call-update) | async-done | bytes 5898256 | tf_op jit(solution)/shard_map/all_gather | solution.py:26
  75.0 5.2 broadcast_in_dim.23
  80.3 116.6 %while.10 = (s32[]{:T(128)}, f32[1024,2880]{1,0:T(8,128)}, s32[]{:T(128)}, s32[1024]{0:T(1024)S(1)}, bf16[1024,2880]{1,0:T(8,128)(2,1)}, /*index=5*/bf16[2880,14...) while((s32[]{:T(128)}, f32[1024,2880]{1,0:T(8,128)}, ...), condition=%wide.region_7.8_spmd, body=%wide.region_5.7_spmd.sunk | while | flops 3186894336 | bytes 38162608 | solution.py:51
  80.3 0.1 compare_select_fusion.5
  80.4 0.1 dynamic_slice.17
  80.4 5.3 gather_fusion
  85.7 7.0 %fusion.24 = f32[128,1440]{0,1:T(8,128)S(1)} fusion(bf16[128,2880]{1,0:T(8,128)(2,1)S(1)} %gather_fusion, bf16[2880,1440]{1,0:T(8,128)(2,1)} %get-tuple-element.160), kind=kOutput, calls=%fused_computation.27.clone.1 | convolution fusion | flops 1061683200 | bytes 9768960 | tf_op jit(solution)/shard_map/while/body/dot_general | solution.py:10
  92.7 14.5 %convolution_multiply_fusion.3 = f32[128,2880]{0,1:T(8,128)S(1)} fusion(bf16[1440,2880]{1,0:T(8,128)(2,1)} %get-tuple-element.162, f32[128]{0:T(128)S(1)} %dynamic_slice.17, bf16[128,2880]{1,0:T(8,128)(2,1)S(1)} %gather_fusion, bf16[2880,1440]{1,0:T(8,128)(2,1)} %get-tuple-element.161, f32[128,1440]{0,1:T(8,128)S(1)} %fusion.24), kind=kOutput, calls=%fused_computation.4.clone.1 | convolution fusion | flops 2124840960 | bytes 19538432 | tf_op jit(solution)/shard_map/while/body/dot_general | solution.py:13
  107.2 0.5 copy.27
  107.7 11.5 %scatter_fusion = f32[1024,2880]{1,0:T(8,128)} fusion(f32[1024,2880]{1,0:T(8,128)} %get-tuple-element.143, s32[128]{0:T(128)S(1)} %compare_select_fusion.5, f32[128,2880]{1,0:T(8,128)S(1)} %copy.27), kind=kCustom, calls=%fused_computation.2.clone.1 | custom fusion | flops 368640 | bytes 4424192 | tf_op jit(solution)/shard_map/while/body/scatter-add | solution.py:49
  119.2 0.1 compare_select_fusion.5
  119.2 0.1 dynamic_slice.17
  119.3 5.3 gather_fusion
  124.6 7.0 %fusion.24 = f32[128,1440]{0,1:T(8,128)S(1)} fusion(bf16[128,2880]{1,0:T(8,128)(2,1)S(1)} %gather_fusion, bf16[2880,1440]{1,0:T(8,128)(2,1)} %get-tuple-element.160), kind=kOutput, calls=%fused_computation.27.clone.1 | convolution fusion | flops 1061683200 | bytes 9768960 | tf_op jit(solution)/shard_map/while/body/dot_general | solution.py:10
  131.6 14.5 %convolution_multiply_fusion.3 = f32[128,2880]{0,1:T(8,128)S(1)} fusion(bf16[1440,2880]{1,0:T(8,128)(2,1)} %get-tuple-element.162, f32[128]{0:T(128)S(1)} %dynamic_slice.17, bf16[128,2880]{1,0:T(8,128)(2,1)S(1)} %gather_fusion, bf16[2880,1440]{1,0:T(8,128)(2,1)} %get-tuple-element.161, f32[128,1440]{0,1:T(8,128)S(1)} %fusion.24), kind=kOutput, calls=%fused_computation.4.clone.1 | convolution fusion | flops 2124840960 | bytes 19538432 | tf_op jit(solution)/shard_map/while/body/dot_general | solution.py:13
  146.1 0.5 copy.27
  146.6 11.5 %scatter_fusion = f32[1024,2880]{1,0:T(8,128)} fusion(f32[1024,2880]{1,0:T(8,128)} %get-tuple-element.143, s32[128]{0:T(128)S(1)} %compare_select_fusion.5, f32[128,2880]{1,0:T(8,128)S(1)} %copy.27), kind=kCustom, calls=%fused_computation.2.clone.1 | custom fusion | flops 368640 | bytes 4424192 | tf_op jit(solution)/shard_map/while/body/scatter-add | solution.py:49
  158.0 0.1 compare_select_fusion.5
  158.1 0.1 dynamic_slice.17
  158.2 5.3 gather_fusion
  163.5 7.0 %fusion.24 = f32[128,1440]{0,1:T(8,128)S(1)} fusion(bf16[128,2880]{1,0:T(8,128)(2,1)S(1)} %gather_fusion, bf16[2880,1440]{1,0:T(8,128)(2,1)} %get-tuple-element.160), kind=kOutput, calls=%fused_computation.27.clone.1 | convolution fusion | flops 1061683200 | bytes 9768960 | tf_op jit(solution)/shard_map/while/body/dot_general | solution.py:10
  170.5 14.5 %convolution_multiply_fusion.3 = f32[128,2880]{0,1:T(8,128)S(1)} fusion(bf16[1440,2880]{1,0:T(8,128)(2,1)} %get-tuple-element.162, f32[128]{0:T(128)S(1)} %dynamic_slice.17, bf16[128,2880]{1,0:T(8,128)(2,1)S(1)} %gather_fusion, bf16[2880,1440]{1,0:T(8,128)(2,1)} %get-tuple-element.161, f32[128,1440]{0,1:T(8,128)S(1)} %fusion.24), kind=kOutput, calls=%fused_computation.4.clone.1 | convolution fusion | flops 2124840960 | bytes 19538432 | tf_op jit(solution)/shard_map/while/body/dot_general | solution.py:13
  185.0 0.5 copy.27
  185.5 11.5 %scatter_fusion = f32[1024,2880]{1,0:T(8,128)} fusion(f32[1024,2880]{1,0:T(8,128)} %get-tuple-element.143, s32[128]{0:T(128)S(1)} %compare_select_fusion.5, f32[128,2880]{1,0:T(8,128)S(1)} %copy.27), kind=kCustom, calls=%fused_computation.2.clone.1 | custom fusion | flops 368640 | bytes 4424192 | tf_op jit(solution)/shard_map/while/body/scatter-add | solution.py:49
  196.9 12.2 %copy.25 = f32[1024,2880]{0,1:T(8,128)} copy(f32[1024,2880]{1,0:T(8,128)} %get-tuple-element.50) | data formatting | bytes 23592960 | tf_op jit(solution)/shard_map/while | solution.py:51
  209.2 0.0 reduce-scatter.2.cloned.1.call-update
  209.2 229.3 %psum.7 = f32[8]{0:T(128)S(1)} all-reduce(f32[8]{0:T(128)S(1)} %get-tuple-element.51), channel_id=1, replica_groups=mesh['dp'=4,'expert'=8] {'dp','expert'}, use_global_device_ids=true, to_apply=%region_10.11 | all-reduce | flops 8 | bytes 64 | tf_op jit(solution)/shard_map/psum | solution.py:56
  438.5 0.5 convert_element_type.50
  439.0 84.4 %reduce-scatter.2.cloned.1.call-done = f32[128,2880]{0,1:T(8,128)} async-done(((f32[1024,2880]{0,1:T(8,128)}), f32[128,2880]{0,1:T(8,128)}) %reduce-scatter.2.cloned.1.call-update) | async-done | bytes 1474576 | tf_op jit(solution)/shard_map/reduce_scatter | solution.py:52
  523.5 2.3 convert_element_type.48
  (8 shorter events, 0.1 us)
Async XLA Ops:
  7.2 67.9 %all-gather.2.cloned.1.call-start = ((), (), s32[]{:S(2)}) async-start(), calls=%async_computation.1 | async-start | bytes 6782976 | tf_op jit(solution)/shard_map/all_gather | solution.py:26
  9.5 514.0 %reduce-scatter.2.cloned.1.call-start = ((), (), s32[]{:S(2)}) async-start(), calls=%async_computation.2 | async-start | bytes 13271040 | tf_op jit(solution)/shard_map/reduce_scatter | solution.py:52
Sparse Core Ops, SparseCore 0:
  9.6 65.3 all-gather.1
  209.3 314.1 reduce-scatter.1
where the time goes:
time: 535 us; the launch traced here: 533 us
  blocking collectives  244 us (46%)
  waiting for transfers between devices  98.9 us (18%)
  local copies, waits for them, and re-layouts  69.9 us (13%)
  matrix products  64.5 us (12%)
  other arithmetic  40.6 us (8%)
  between operations  14.8 us (3%)
    psum x1, blocking collectives, shards(): expert_load = lax.psum(local_load, ('dp', 'expert')).astype(jnp.int32)  229 us
    reduce_scatter x1, waiting for transfers between devices, shards(): lax.psum_scatter(partial_value, 'expert', scatter_dimension=0, tiled=True)  84.4 us
    dot_general x3, matrix products, expert_ffn(): return jnp.dot(hidden, down_mat, preferred_element_type=jnp.float32)  43.6 us
    scatter-add x3, other arithmetic, per_block(): return partial_value.at[rows_idx].add(result * weight[:, None])  34.4 us
    unnamed x3, local copies, waits for them, and re-layouts  25.9 us
    dot_general x3, matrix products, expert_ffn(): gate_val = jnp.dot(rows, gate_mat, preferred_element_type=jnp.float32)  20.9 us
    gather x3, local copies, waits for them, and re-layouts, per_block(): result = expert_ffn(gathered[rows_idx], gate_mat, up_mat, down_mat)  15.9 us
    all_gather x1, blocking collectives, shards(): lax.all_gather(table.astype(jnp.bfloat16), 'expert', axis=0, tiled=True)  14.5 us
  transfers between devices with their start and end apart: 2, of which 2 were waited for; matrix products, arithmetic and copies ran while one was open for 7% of the time, Pallas kernels for 0%

commit v1 on v0

v1 whole, which is shorter than its diff:
```python
import functools

import jax
import jax.numpy as jnp
from jax import lax
from jax.experimental import pallas as pl
from jax.experimental.pallas import tpu as pltpu
from jax.sharding import PartitionSpec as P

MESH = pl.DeviceIdType.MESH
LANES = 128
PIECES = 2
FF_TILE = 512
OUT_TILE = 512


def tiles(total, size):
    return [(at, min(size, total - at)) for at in range(0, total, size)]


def kernel(
    chips, n_dp, ext_hbm, wg_hbm, wu_hbm, wd_hbm, out_hbm, load_ref,
    tok, wg, wu, wd, hidden, own, sib_out, sib_in, sums_in, counts,
    tok_recv, pair_recv, send_right, send_left, send_pair, sib_send, sib_recv,
    sums_recv, sums_send, w_sem, local_sem, count_send, count_recv,
):
    rows = tok.shape[1] // 2
    width = wd.shape[1]
    ff = wd.shape[0]
    tail_at = tok.shape[2] - LANES
    gate_lane = width - tail_at
    piece = rows // PIECES
    e = lax.axis_index("expert")
    group = lax.axis_index("dp")
    pos = e // 2
    lane = e % 2
    pair = {"expert": e + 1 - 2 * lane}
    right = {"expert": e + 2}
    left = {"expert": e - 2}
    has_left = pos > 0
    has_right = pos < chips - 1
    middle = jnp.logical_and(has_left, has_right)

    weights = [
        pltpu.make_async_copy(src, dst, w_sem.at[i])
        for i, (src, dst) in enumerate(((wg_hbm, wg), (wu_hbm, wu), (wd_hbm, wd)))
    ]
    mine = pltpu.make_async_copy(ext_hbm, tok.at[pos, pl.ds(0, rows)], local_sem.at[0])
    mine.start()
    for copy in weights:
        copy.start()

    barrier = pltpu.get_barrier_semaphore()
    pl.semaphore_signal(barrier, inc=1, device_id=pair, device_id_type=MESH)
    for i in range(1, n_dp):
        peer = {"dp": (group + i) % n_dp}
        pl.semaphore_signal(barrier, inc=1, device_id=peer, device_id_type=MESH)

    @pl.when(has_left)
    def _():
        pl.semaphore_signal(barrier, inc=1, device_id=left, device_id_type=MESH)

    @pl.when(has_right)
    def _():
        pl.semaphore_signal(barrier, inc=1, device_id=right, device_id_type=MESH)

    neighbours = (pos + chips - 1) // chips + (2 * chips - 2 - pos) // chips
    pl.semaphore_wait(barrier, n_dp + neighbours)

    def tok_copy(d, target, send, to_pair=False):
        return pltpu.make_async_remote_copy(
            src_ref=tok.at[d, pl.ds(0, rows)],
            dst_ref=tok.at[d, pl.ds(rows if to_pair else 0, rows)],
            send_sem=send.at[d],
            recv_sem=(pair_recv if to_pair else tok_recv).at[d],
            device_id=target,
            device_id_type=MESH,
        )

    def sib_copy(d):
        return pltpu.make_async_remote_copy(
            src_ref=sib_out.at[d],
            dst_ref=sib_in.at[d],
            send_sem=sib_send.at[d],
            recv_sem=sib_recv.at[d],
            device_id=pair,
            device_id_type=MESH,
        )

    def sum_copy(d, q, slot, target):
        part = pl.ds(q * piece, piece)
        return pltpu.make_async_remote_copy(
            src_ref=sib_out.at[d, part],
            dst_ref=sums_in.at[slot, part],
            send_sem=sums_send.at[d, q],
            recv_sem=sums_recv.at[slot, q],
            device_id=target,
            device_id_type=MESH,
        )

    def send_sum(d, q):
        @pl.when(d > pos)
        def _():
            sum_copy(d, q, d + 1, right).start()

        @pl.when(d < pos)
        def _():
            sum_copy(d, q, d, left).start()

    def pair_sum(d, part):
        return own[d, part].astype(jnp.float32) + sib_in[d, part].astype(jnp.float32)

    def compute(d):
        x = tok.at[d]
        tail = x[:, pl.ds(tail_at, LANES)].astype(jnp.float32)
        at = lax.broadcasted_iota(jnp.int32, tail.shape, 1)
        column = jnp.sum(jnp.where(at == gate_lane + e, tail, 0.0), axis=1, keepdims=True)
        counts[group] += jnp.sum(jnp.where(tail > 0, 1.0, 0.0), axis=0, keepdims=True)
        for start, size in tiles(ff, FF_TILE):
            cols = pl.ds(start, size)
            g = jnp.dot(x[:, pl.ds(0, width)], wg[:, cols], preferred_element_type=jnp.float32)
            u = jnp.dot(x[:, pl.ds(0, width)], wu[:, cols], preferred_element_type=jnp.float32)
            hidden[:, cols] = (g / (1.0 + jnp.exp(-g)) * u).astype(jnp.bfloat16)
        for start, size in tiles(width, OUT_TILE):
            cols = pl.ds(start, size)
            y = jnp.dot(hidden[...], wd[:, cols], preferred_element_type=jnp.float32) * column
            own[d, :, cols] = y[:rows].astype(own.dtype)
            sib_out[d, :, cols] = y[rows:].astype(jnp.bfloat16)
        sib_copy(d).start()

    def arrive(d):
        tok_copy(d, pair, send_pair).wait_recv()

        @pl.when(jnp.logical_and(d < pos, has_right))
        def _():
            tok_copy(d, right, send_right).start()

        @pl.when(jnp.logical_and(d > pos, has_left))
        def _():
            tok_copy(d, left, send_left).start()

        tok_copy(d, pair, send_pair, True).start()

    counts[group] = jnp.zeros((1, LANES), jnp.float32)
    mine.wait()

    @pl.when(has_right)
    def _():
        tok_copy(pos, right, send_right).start()

    @pl.when(has_left)
    def _():
        tok_copy(pos, left, send_left).start()

    tok_copy(pos, pair, send_pair, True).start()
    for copy in weights:
        copy.wait()

    def step(t, carry):
        far = (t + 1) // 2
        d = pos + (1 - 2 * (t % 2)) * far

        @pl.when(t % 2 == 1)
        def _():
            @pl.when(pos - far >= 0)
            def _():
                arrive(pos - far)

            @pl.when(pos + far < chips)
            def _():
                arrive(pos + far)

        @pl.when(jnp.logical_and(d >= 0, d < chips))
        def _():
            tok_copy(d, pair, send_pair, True).wait_recv()
            compute(d)

            @pl.when(jnp.logical_and(t > 0, jnp.logical_not(middle)))
            def _():
                sib_copy(d).wait()
                for q in range(PIECES):
                    part = pl.ds(q * piece, piece)
                    sib_out[d, part] = pair_sum(d, part).astype(jnp.bfloat16)
                    send_sum(d, q)

        return carry

    lax.fori_loop(0, 2 * chips - 1, step, 0)

    def count_copy(i, slot):
        return pltpu.make_async_remote_copy(
            src_ref=counts.at[group],
            dst_ref=counts.at[slot],
            send_sem=count_send.at[i],
            recv_sem=count_recv.at[slot],
            device_id={"dp": (group + i) % n_dp},
            device_id_type=MESH,
        )

    for i in range(1, n_dp):
        count_copy(i, group).start()

    @pl.when(middle)
    def _():
        def forward(u, carry):
            late = (2 * pos) // chips
            past_right = (pos + 1 + u) // chips
            past_left = (u + chips - pos) // chips
            rights_first = (1 - past_right) * (pos + 1 + u) + past_right * (chips - 2 - u)
            lefts_first = (1 - past_left) * (pos - 1 - u) + past_left * (u + 1)
            d = (1 - late) * rights_first + late * lefts_first
            slot = d + (d + chips - pos) // chips
            sib_copy(d).wait()
            for q in range(PIECES):
                part = pl.ds(q * piece, piece)
                sum_copy(d, q, slot, pair).wait_recv()
                total = pair_sum(d, part) + sums_in[slot, part].astype(jnp.float32)
                sib_out[d, part] = total.astype(jnp.bfloat16)
                send_sum(d, q)
            return carry

        lax.fori_loop(0, chips - 1, forward, 0)

    sib_copy(pos).wait()
    for q in range(PIECES):
        part = pl.ds(q * piece, piece)

        def from_left(q=q, part=part):
            sum_copy(pos, q, pos + 1, pair).wait_recv()
            return sums_in[pos + 1, part].astype(jnp.float32)

        def from_right(q=q, part=part):
            sum_copy(pos, q, pos, pair).wait_recv()
            return sums_in[pos, part].astype(jnp.float32)

        @pl.when(middle)
        def _():
            total = pair_sum(pos, part) + from_left() + from_right()
            sib_out[pos, part] = total.astype(jnp.bfloat16)

        @pl.when(jnp.logical_not(has_left))
        def _():
            sib_out[pos, part] = (pair_sum(pos, part) + from_right()).astype(jnp.bfloat16)

        @pl.when(jnp.logical_not(has_right))
        def _():
            sib_out[pos, part] = (pair_sum(pos, part) + from_left()).astype(jnp.bfloat16)

    result = pltpu.make_async_copy(sib_out.at[pos], out_hbm, local_sem.at[1])
    result.start()

    load = counts[group]
    for i in range(1, n_dp):
        count_copy(i, (group + i) % n_dp).wait_recv()
        load = load + counts[(group + i) % n_dp]
    load_ref[...] = load
    for i in range(1, n_dp):
        count_copy(i, group).wait_send()

    def drain(d, carry):
        tok_copy(d, pair, send_pair, True).wait_send()

        @pl.when(jnp.logical_and(d <= pos, has_right))
        def _():
            tok_copy(d, right, send_right).wait_send()

        @pl.when(jnp.logical_and(d >= pos, has_left))
        def _():
            tok_copy(d, left, send_left).wait_send()

        for q in range(PIECES):

            @pl.when(d > pos)
            def _():
                sum_copy(d, q, d, right).wait_send()

            @pl.when(d < pos)
            def _():
                sum_copy(d, q, d, left).wait_send()

        return carry

    lax.fori_loop(0, chips, drain, 0)
    result.wait()


def shards(n_dp, n_experts, tokens, expert_ids, gates, w_gate, w_up, w_down):
    rows, width = tokens.shape
    ff = w_gate.shape[2]
    chips = n_experts // 2
    full = -(-(width + n_experts) // LANES) * LANES
    experts = jnp.arange(n_experts, dtype=jnp.int32)
    onehot = expert_ids[:, :, None] == experts[None, None, :]
    table = jnp.sum(gates.astype(jnp.float32)[:, :, None] * onehot.astype(jnp.float32), axis=1)
    blank = jnp.zeros((rows, full - width - n_experts), jnp.bfloat16)
    ext = jnp.concatenate([tokens, table.astype(jnp.bfloat16), blank], axis=1)
    bf16 = jnp.bfloat16
    dma = pltpu.SemaphoreType.DMA
    flops = 2 * chips * 2 * rows * 3 * width * ff
    mixed, load = pl.pallas_call(
        functools.partial(kernel, chips, n_dp),
        out_shape=(
            jax.ShapeDtypeStruct((rows, width), bf16),
            jax.ShapeDtypeStruct((1, LANES), jnp.float32),
        ),
        in_specs=[pl.BlockSpec(memory_space=pl.ANY)] * 4,
        out_specs=(
            pl.BlockSpec(memory_space=pl.ANY),
            pl.BlockSpec(memory_space=pltpu.VMEM),
        ),
        scratch_shapes=[
            pltpu.VMEM((chips, 2 * rows, full), bf16),
            pltpu.VMEM((width, ff), bf16),
            pltpu.VMEM((width, ff), bf16),
            pltpu.VMEM((ff, width), bf16),
            pltpu.VMEM((2 * rows, ff), bf16),
            pltpu.VMEM((chips, rows, width), jnp.float32 if chips <= 4 else bf16),
            pltpu.VMEM((chips, rows, width), bf16),
            pltpu.VMEM((chips, rows, width), bf16),
            pltpu.VMEM((chips + 1, rows, width), bf16),
            pltpu.VMEM((n_dp, 1, LANES), jnp.float32),
            dma((chips,)),
            dma((chips,)),
            dma((chips,)),
            dma((chips,)),
            dma((chips,)),
            dma((chips,)),
            dma((chips,)),
            dma((chips + 1, PIECES)),
            dma((chips, PIECES)),
            dma((3,)),
            dma((2,)),
            dma((n_dp,)),
            dma((n_dp,)),
        ],
        compiler_params=pltpu.CompilerParams(
            collective_id=0, has_side_effects=True, vmem_limit_bytes=(64 << 20) - (256 << 10)
        ),
        cost_estimate=pl.CostEstimate(
            flops=flops, bytes_accessed=6 * width * ff, transcendentals=4 * chips * rows * ff
        ),
    )(ext, w_gate[0], w_up[0], w_down[0])
    gate_lane = width - (full - LANES)
    return mixed, load[0, gate_lane : gate_lane + n_experts].astype(jnp.int32)


def solution(mesh):
    placed = (
        P(("dp", "expert"), None),
        P(("dp", "expert"), None),
        P(("dp", "expert"), None),
        P("expert", None, None),
        P("expert", None, None),
        P("expert", None, None),
    )
    return jax.shard_map(
        functools.partial(shards, mesh.shape["dp"], mesh.shape["expert"]),
        mesh=mesh,
        in_specs=placed,
        out_specs=(P(("dp", "expert"), None), P()),
        check_vma=False,
    )
```

time: 535 us -> 146 us (0.27)
  blocking collectives: 244 us -> 0 us
  Pallas kernels: 0 us -> 114 us
  waiting for transfers between devices: 98.9 us -> 0 us
  matrix products: 64.5 us -> 0 us
  local copies, waits for them, and re-layouts: 69.9 us -> 28.4 us
  other arithmetic: 40.6 us -> 2.55 us
  between operations: 14.8 us -> 0.65 us
    psum x1 -> x0, blocking collectives: 229 us -> none  [shards(): expert_load = lax.psum(local_load, ('dp', 'expert')).astype(jnp.int32)]
    pallas_call x0 -> x1, Pallas kernels: none -> 114 us  [shards(): pl.pallas_call(functools.partial(kernel, chips, n_dp), out_shape=(jax.Sha...]
    reduce_scatter x1 -> x0, waiting for transfers between devices: 84.4 us -> none  [shards(): lax.psum_scatter(partial_value, 'expert', scatter_dimension=0, tiled=True)]
    dot_general x6 -> x0, matrix products: 64.5 us -> none  [the longest x3 43.6 us: expert_ffn(): return jnp.dot(hidden, down_mat, preferred_element_type=jnp.float32)]
    scatter-add x3 -> x0, other arithmetic: 34.4 us -> none  [per_block(): return partial_value.at[rows_idx].add(result * weight[:, None])]
    gather x4 -> x0, local copies, waits for them, and re-layouts: 20.4 us -> none  [the longest x3 15.9 us: per_block(): result = expert_ffn(gathered[rows_idx], gate_mat, up_mat, down_mat)]
    all_gather x1 -> x0, blocking collectives: 14.5 us -> none  [shards(): lax.all_gather(table.astype(jnp.bfloat16), 'expert', axis=0, tiled=True)]
    all_gather x1 -> x0, waiting for transfers between devices: 14.5 us -> none  [shards(): lax.all_gather(tokens, 'expert', axis=0, tiled=True)]
  transfers between devices with their start and end apart: 2 -> 0, of which waited for: 2 -> 0; matrix products, arithmetic and copies ran while one was open for 7% -> 0% of each run, Pallas kernels for 0% -> 0%
where the time goes in v1:
time: 146 us
  Pallas kernels  114 us (78%)
  local copies, waits for them, and re-layouts  28.4 us (19%)
  other arithmetic  2.55 us (2%)
    pallas_call x1, Pallas kernels, shards(): pl.pallas_call(functools.partial(kernel, chips, n_dp), out_shape=(jax.Sha...  114 us
    unnamed x4, local copies, waits for them, and re-layouts  27.2 us

profile of v1, /device:TPU:0, one launch (start us, length us, event | category | flops | bytes accessed | tf_op | source)
XLA Modules:
  0.0 145.6 jit_solution(2176429068603268017)
XLA Ops:
  0.6 0.7 convert_element_type.13
  1.3 0.7 select_reduce_fusion
  2.0 0.1 copy.15
  2.1 1.5 copy.14
  3.6 1.1 concatenate.3.ext_hbm
  4.7 11.7 %copy.16 = bf16[1,2880,1440]{2,1,0:T(8,128)(2,1)} copy(bf16[1,2880,1440]{1,2,0:T(8,128)(2,1)} %param.9) | data formatting | bytes 16588800 | tf_op args[3]
  16.4 11.8 %copy.17 = bf16[1,2880,1440]{2,1,0:T(8,128)(2,1)} copy(bf16[1,2880,1440]{1,2,0:T(8,128)(2,1)} %param.10) | data formatting | bytes 16588800 | tf_op args[4]
  28.2 114.0 %shard_map.77 = (bf16[128,2880]{1,0:T(8,128)(2,1)}, f32[1,128]{1,0:T(1,128)}) custom-call(bf16[128,2944]{1,0:T(8,128)(2,1)} %concatenate.3.ext_hbm, bf16[2880,1440]{1,0:T(8,128)(2,1)} %bitcast.5, bf16[2880,1440]{1,0:T(8,128)(2,1)} %bitcast.6, bf16[1440,2880]{1,0:T(8,128)(2,1)} %bitcast.7), custom_call_target="tpu_custom_call" | custom-call | flops 25480396800 | bytes 24883200 | tf_op jit(solution)/shard_map/pallas_call | solution.py:300
  142.1 2.3 %copy.18 = bf16[128,2880]{0,1:T(8,128)(2,1)} copy(bf16[128,2880]{1,0:T(8,128)(2,1)} %get-tuple-element.8) | data formatting | bytes 1474560
  144.4 1.2 convert_bitcast_fusion
  (1 shorter events, 0.0 us)

commit v2 on v1

--- a/solution.py
+++ b/solution.py
@@ -9,13 +9,17 @@
 
 MESH = pl.DeviceIdType.MESH
 LANES = 128
-PIECES = 2
+PIECES = 4
 FF_TILE = 512
 OUT_TILE = 512
 
 
 def tiles(total, size):
     return [(at, min(size, total - at)) for at in range(0, total, size)]
+
+
+def dot_rows(a, b):
+    return lax.dot_general(a, b, (((1,), (1,)), ((), ())), preferred_element_type=jnp.float32)
 
 
 def kernel(
@@ -118,8 +122,8 @@
         counts[group] += jnp.sum(jnp.where(tail > 0, 1.0, 0.0), axis=0, keepdims=True)
         for start, size in tiles(ff, FF_TILE):
             cols = pl.ds(start, size)
-            g = jnp.dot(x[:, pl.ds(0, width)], wg[:, cols], preferred_element_type=jnp.float32)
-            u = jnp.dot(x[:, pl.ds(0, width)], wu[:, cols], preferred_element_type=jnp.float32)
+            g = dot_rows(x[:, pl.ds(0, width)], wg[cols])
+            u = dot_rows(x[:, pl.ds(0, width)], wu[cols])
             hidden[:, cols] = (g / (1.0 + jnp.exp(-g)) * u).astype(jnp.bfloat16)
         for start, size in tiles(width, OUT_TILE):
             cols = pl.ds(start, size)
@@ -157,10 +161,10 @@
         copy.wait()
 
     def step(t, carry):
-        far = (t + 1) // 2
+        far = ((t + 1) // 2) % chips
         d = pos + (1 - 2 * (t % 2)) * far
 
-        @pl.when(t % 2 == 1)
+        @pl.when(jnp.logical_and(t % 2 == 1, t < 2 * chips - 1))
         def _():
             @pl.when(pos - far >= 0)
             def _():
@@ -175,7 +179,7 @@
             tok_copy(d, pair, send_pair, True).wait_recv()
             compute(d)
 
-            @pl.when(jnp.logical_and(t > 0, jnp.logical_not(middle)))
+            @pl.when(jnp.logical_and(t < 2 * chips - 1, jnp.logical_not(middle)))
             def _():
                 sib_copy(d).wait()
                 for q in range(PIECES):
@@ -185,7 +189,7 @@
 
         return carry
 
-    lax.fori_loop(0, 2 * chips - 1, step, 0)
+    lax.fori_loop(1, 2 * chips, step, 0)
 
     def count_copy(i, slot):
         return pltpu.make_async_remote_copy(
@@ -310,8 +314,8 @@
         ),
         scratch_shapes=[
             pltpu.VMEM((chips, 2 * rows, full), bf16),
-            pltpu.VMEM((width, ff), bf16),
-            pltpu.VMEM((width, ff), bf16),
+            pltpu.VMEM((ff, width), bf16),
+            pltpu.VMEM((ff, width), bf16),
             pltpu.VMEM((ff, width), bf16),
             pltpu.VMEM((2 * rows, ff), bf16),
             pltpu.VMEM((chips, rows, width), jnp.float32 if chips <= 4 else bf16),
@@ -339,7 +343,7 @@
         cost_estimate=pl.CostEstimate(
             flops=flops, bytes_accessed=6 * width * ff, transcendentals=4 * chips * rows * ff
         ),
-    )(ext, w_gate[0], w_up[0], w_down[0])
+    )(ext, w_gate[0].T, w_up[0].T, w_down[0])
     gate_lane = width - (full - LANES)
     return mixed, load[0, gate_lane : gate_lane + n_experts].astype(jnp.int32)
 

time: 146 us -> 121 us (0.83)
  local copies, waits for them, and re-layouts: 28.4 us -> 4.89 us
    unnamed x4 -> x2, local copies, waits for them, and re-layouts: 27.2 us -> 3.71 us
where the time goes in v2:
time: 121 us
  Pallas kernels  113 us (93%)
  local copies, waits for them, and re-layouts  4.89 us (4%)
  other arithmetic  2.62 us (2%)
    pallas_call x1, Pallas kernels, shards(): pl.pallas_call(functools.partial(kernel, chips, n_dp), out_shape=(jax.Sha...  113 us
    unnamed x2, local copies, waits for them, and re-layouts  3.71 us

profile of v2, /device:TPU:0, one launch (start us, length us, event | category | flops | bytes accessed | tf_op | source)
XLA Modules:
  0.0 121.1 jit_solution(13403538046221285727)
XLA Ops:
  0.6 0.7 convert_element_type.13
  1.3 0.7 select_reduce_fusion
  2.0 0.1 copy.13
  2.1 1.5 %copy.12 = bf16[128,2880]{1,0:T(8,128)(2,1)S(1)} copy(bf16[128,2880]{0,1:T(8,128)(2,1)} %param.6) | data formatting | bytes 1474560 | tf_op args[0]
  3.6 1.0 concatenate.3.ext_hbm
  4.6 113.0 %shard_map.77 = (bf16[128,2880]{1,0:T(8,128)(2,1)}, f32[1,128]{1,0:T(1,128)}) custom-call(bf16[128,2944]{1,0:T(8,128)(2,1)} %concatenate.3.ext_hbm, bf16[1440,2880]{1,0:T(8,128)(2,1)} %bitcast.9, bf16[1440,2880]{1,0:T(8,128)(2,1)} %bitcast.10, bf16[1440,2880]{1,0:T(8,128)(2,1)} %bitcast.11), custom_call_target="tpu_custom_call" | custom-call | flops 25480396800 | bytes 24883200 | tf_op jit(solution)/shard_map/pallas_call | solution.py:304
  117.6 2.3 %copy.14 = bf16[128,2880]{0,1:T(8,128)(2,1)} copy(bf16[128,2880]{1,0:T(8,128)(2,1)} %get-tuple-element.8) | data formatting | bytes 1474560
  119.9 1.2 %convert_bitcast_fusion = s32[8]{0:T(128)} fusion(f32[1,128]{1,0:T(1,128)} %get-tuple-element.5), kind=kLoop, calls=%fused_computation.2 | loop fusion | flops 8 | bytes 64 | tf_op jit(solution)/shard_map/convert_element_type | solution.py:348
  (1 shorter events, 0.0 us)

commit v3 on v2

--- a/solution.py
+++ b/solution.py
@@ -145,6 +145,15 @@
 
         tok_copy(d, pair, send_pair, True).start()
 
+    def arrivals(far):
+        @pl.when(pos - far >= 0)
+        def _():
+            arrive(pos - far)
+
+        @pl.when(pos + far < chips)
+        def _():
+            arrive(pos + far)
+
     counts[group] = jnp.zeros((1, LANES), jnp.float32)
     mine.wait()
 
@@ -164,15 +173,9 @@
         far = ((t + 1) // 2) % chips
         d = pos + (1 - 2 * (t % 2)) * far
 
-        @pl.when(jnp.logical_and(t % 2 == 1, t < 2 * chips - 1))
-        def _():
-            @pl.when(pos - far >= 0)
-            def _():
-                arrive(pos - far)
-
-            @pl.when(pos + far < chips)
-            def _():
-                arrive(pos + far)
+        @pl.when(jnp.logical_or(t == 1, jnp.logical_and(t % 2 == 0, middle)))
+        def _():
+            arrivals(t // 2 + 1)
 
         @pl.when(jnp.logical_and(d >= 0, d < chips))
         def _():
@@ -186,6 +189,10 @@
                     part = pl.ds(q * piece, piece)
                     sib_out[d, part] = pair_sum(d, part).astype(jnp.bfloat16)
                     send_sum(d, q)
+
+        @pl.when(jnp.logical_and(t % 2 == 0, jnp.logical_not(middle)))
+        def _():
+            arrivals(t // 2 + 1)
 
         return carry
 

time: 121 us -> 121 us (level)
  no operation moved by 1% of the time
where the time goes in v3:
time: 121 us
  Pallas kernels  113 us (93%)
  local copies, waits for them, and re-layouts  4.89 us (4%)
  other arithmetic  2.62 us (2%)
    pallas_call x1, Pallas kernels, shards(): pl.pallas_call(functools.partial(kernel, chips, n_dp), out_shape=(jax.Sha...  113 us
    unnamed x2, local copies, waits for them, and re-layouts  3.71 us

profile of v3, /device:TPU:0, one launch (start us, length us, event | category | flops | bytes accessed | tf_op | source)
XLA Modules:
  0.0 121.1 jit_solution(5830387479897236608)
XLA Ops:
  0.6 0.7 convert_element_type.13
  1.3 0.7 select_reduce_fusion
  2.0 0.1 copy.13
  2.1 1.5 %copy.12 = bf16[128,2880]{1,0:T(8,128)(2,1)S(1)} copy(bf16[128,2880]{0,1:T(8,128)(2,1)} %param.6) | data formatting | bytes 1474560 | tf_op args[0]
  3.6 1.0 concatenate.3.ext_hbm
  4.6 113.0 %shard_map.77 = (bf16[128,2880]{1,0:T(8,128)(2,1)}, f32[1,128]{1,0:T(1,128)}) custom-call(bf16[128,2944]{1,0:T(8,128)(2,1)} %concatenate.3.ext_hbm, bf16[1440,2880]{1,0:T(8,128)(2,1)} %bitcast.9, bf16[1440,2880]{1,0:T(8,128)(2,1)} %bitcast.10, bf16[1440,2880]{1,0:T(8,128)(2,1)} %bitcast.11), custom_call_target="tpu_custom_call" | custom-call | flops 25480396800 | bytes 24883200 | tf_op jit(solution)/shard_map/pallas_call | solution.py:311
  117.6 2.3 %copy.14 = bf16[128,2880]{0,1:T(8,128)(2,1)} copy(bf16[128,2880]{1,0:T(8,128)(2,1)} %get-tuple-element.8) | data formatting | bytes 1474560
  119.9 1.2 %convert_bitcast_fusion = s32[8]{0:T(128)} fusion(f32[1,128]{1,0:T(1,128)} %get-tuple-element.5), kind=kLoop, calls=%fused_computation.2 | loop fusion | flops 8 | bytes 64 | tf_op jit(solution)/shard_map/convert_element_type | solution.py:355
  (1 shorter events, 0.0 us)
